TPU v7x, 32 devices: a whole 2x2x4 slice. The times are simulated.
32 devices in a mesh: grp: 2 (over y), bus: 4 (over z), line: 2 (over x), scen: 2 (over core).
Axes of the slice: x: 2, y: 2, z: 4, core: 2. Of those that a mesh axis runs over, the one named last changes fastest.
Arguments:
- injections: float32 [128, 4, 4096], P(('grp', 'bus', 'scen'), None, 'line'), parts along dimension 0, may hold values from -6 to 6
- shift_factors: float32 [8192, 16384], P('line', 'bus'), may hold values from -0.046875 to 0.046875
- line_limits: int32 [8192], P('line'), may hold values from 20 to 149
- overload_cost: float32 [8192], P('line'), may hold values from 0.5 to 5
Outputs:
- line_flows: float32 [128, 8192], P(('grp', 'bus', 'scen'), 'line'), parts along dimension 0
- penalty_gradient: float32 [128, 4, 4096], P(('grp', 'bus', 'scen'), None, 'line'), parts along dimension 0
There are 2 independent parts, one for each index of `grp`. A program takes and returns all parts, laid end to end along the dimension named above; an argument that names none is the same for every part. Nothing has to cross between parts.
Inputs may be any that keep to these rules, and one draw needn't show every extreme that they name: `line_limits`: thermal limits in MW on a 100 MW base.
All inputs are finite; a program needn't handle non-finite values.
Results may differ from a plain program's by a relative error of at most 0.00011.
Values sent between devices are 32-bit elements; how exact they have to be, the bound alone decides.
A program may use at most 128 MiB of HBM per device.

v0:
```python
import jax
import jax.numpy as jnp
from jax import lax
from jax.sharding import PartitionSpec as P


def contract_buses(values, factors):
    return lax.dot_general(
        values,
        factors,
        (((1,), (1,)), ((), ())),
        precision=lax.Precision.HIGHEST,
        preferred_element_type=jnp.float32,
    )


def penalty_slopes(flows_part, line_limits, overload_cost):
    limits = line_limits.astype(jnp.float32) / 100.0
    excess = jax.nn.relu(flows_part - limits) - jax.nn.relu(-flows_part - limits)
    return 2.0 * overload_cost * excess


def on_device(injections, shift_factors, line_limits, overload_cost):
    widened = lax.all_gather(injections, "line", axis=2, tiled=True)
    relayed = lax.all_to_all(widened, "bus", split_axis=1, concat_axis=0, tiled=True)
    partial_flows = contract_buses(relayed[:, 0, :], shift_factors)
    group_rows = partial_flows.shape[0]
    own_count = group_rows // lax.axis_size("bus")
    summed = lax.psum(partial_flows, "bus")
    group_slopes = penalty_slopes(summed, line_limits, overload_cost)
    line_flows = lax.dynamic_slice_in_dim(summed, lax.axis_index("bus") * own_count, own_count, 0)
    partial_grad = jnp.dot(
        group_slopes,
        shift_factors,
        precision=lax.Precision.HIGHEST,
        preferred_element_type=jnp.float32,
    )
    reduced = lax.psum_scatter(partial_grad, "line", scatter_dimension=1, tiled=True)
    penalty_gradient = lax.all_to_all(
        reduced[:, None, :], "bus", split_axis=0, concat_axis=1, tiled=True
    )
    return (line_flows, penalty_gradient)


def solution(mesh):
    in_specs = (P(("grp", "bus", "scen"), None, "line"), P("line", "bus"), P("line"), P("line"))
    out_specs = (P(("grp", "bus", "scen"), "line"), P(("grp", "bus", "scen"), None, "line"))
    return jax.shard_map(
        on_device, mesh=mesh, in_specs=in_specs, out_specs=out_specs, check_vma=False
    )
```

profile of v0, /device:TPU:0, one launch (start us, length us, event | category | flops | bytes accessed | tf_op | source)
XLA Modules:
  0.0 223.7 jit_solution(5629796355818969370)
XLA Ops:
  7.2 0.0 copy-start.1
  7.2 0.0 copy-start
  7.2 0.0 all-reduce.2.cloned.1.call-start
  7.2 1.1 copy.9
  8.3 9.9 %all_gather.3 = f32[8,4,4096]{2,0,1:T(8,128)S(1)} all-gather(f32[8,4,2048]{2,0,1:T(8,128)S(1)} %copy.9), channel_id=1, replica_groups=mesh['grp'=2,'bus'=4,'line'=2,'scen'=2] {'line'}, dimensions={2}, use_global_device_ids=true | all-gather | bytes 786432 | tf_op jit(solution)/shard_map/all_gather | solution.py:24
  18.2 18.5 %all_to_all.33 = f32[8,4,4096]{2,0,1:T(8,128)S(1)} all-to-all(f32[8,4,4096]{2,0,1:T(8,128)S(1)} %all_gather.3), channel_id=1, replica_groups=mesh['grp'=2,'bus'=4,'line'=2,'scen'=2] {'bus'}, dimensions={1} | all-to-all | bytes 1048576 | tf_op jit(solution)/shard_map/all_to_all | solution.py:25
  36.8 66.5 %fusion = f32[32,4096]{1,0:T(8,128)} fusion(f32[4096,4096]{1,0:T(8,128)} %param.5, f32[8,4,4096]{2,0,1:T(8,128)S(1)} %all_to_all.33), kind=kOutput, calls=%fused_computation | convolution fusion | flops 6442450944 | bytes 68157440 | tf_op jit(solution)/shard_map/dot_general | solution.py:8
  103.3 0.0 all-reduce.2.cloned.1.call-update
  103.3 0.2 reduce-scatter.2.cloned.1.call-start
  103.6 0.0 copy-done.1
  103.6 0.0 copy-done
  103.6 37.3 %all-reduce.2.cloned.1.call-done = f32[32,4096]{1,0:T(8,128)} async-done(((f32[32,4096]{1,0:T(8,128)}), f32[32,4096]{1,0:T(8,128)}) %all-reduce.2.cloned.1.call-update) | async-done | bytes 524304 | tf_op jit(solution)/shard_map/psum | solution.py:29
  140.9 44.9 %fusion.2 = f32[32,4096]{1,0:T(8,128)} fusion(f32[4096,4096]{1,0:T(8,128)} %param.5, f32[32,4096]{1,0:T(8,128)} %all-reduce.2.cloned.1.call-done, f32[4096]{0:T(1024)S(1)} %get-tuple-element.2, f32[4096]{0:T(1024)S(1)} %get-tuple-element.3), kind=kOutput, calls=%fused_computation.2 | convolution fusion | flops 6443368448 | bytes 68190208 | tf_op jit(solution)/shard_map/dot_general | solution.py:32
  185.8 0.0 reduce-scatter.2.cloned.1.call-update
  185.9 14.7 %reduce-scatter.2.cloned.1.call-done = f32[32,2048]{1,0:T(8,128)} async-done(((f32[32,4096]{1,0:T(8,128)}), f32[32,2048]{1,0:T(8,128)}) %reduce-scatter.2.cloned.1.call-update) | async-done | bytes 262160 | tf_op jit(solution)/shard_map/reduce_scatter | solution.py:38
  200.5 1.9 copy.10
  202.5 4.6 %all-to-all-start.1 = ((f32[32,1,2048]{2,1,0:T(1,128)}), f32[32,1,2048]{2,1,0:T(1,128)S(1)}, u32[]{:S(2)}, u32[]{:S(2)}) async-start(f32[32,1,2048]{2,1,0:T(1,128)} %copy.10), calls=%async_computation.2 | async-start | bytes 524288 | tf_op jit(solution)/shard_map/all_to_all | solution.py:39
  207.1 1.6 constant_dynamic-slice_fusion
  208.6 7.3 %all-to-all-done.1 = f32[32,1,2048]{2,1,0:T(1,128)S(1)} async-done(((f32[32,1,2048]{2,1,0:T(1,128)}), f32[32,1,2048]{2,1,0:T(1,128)S(1)}, u32[]{:S(2)}, u32[]{:S(2)}) %all-to-all-start.1) | async-done | bytes 262176 | tf_op jit(solution)/shard_map/all_to_all | solution.py:39
  216.0 0.9 copy.13
  (1 shorter events, 0.0 us)
Async XLA Ops:
  7.2 96.4 %copy-start.1 = (f32[4096]{0:T(1024)S(1)}, f32[4096]{0:T(1024)}, u32[]{:S(2)}) copy-start(f32[4096]{0:T(1024)} %param.7) | copy-start | bytes 49156
  7.2 96.4 %copy-start = (s32[4096]{0:T(1024)S(1)}, s32[4096]{0:T(1024)}, u32[]{:S(2)}) copy-start(s32[4096]{0:T(1024)} %param.6) | copy-start | bytes 49156
  7.2 133.7 %all-reduce.2.cloned.1.call-start = ((), (), s32[]{:S(2)}) async-start(), calls=%async_computation.3 | async-start | bytes 1048576 | tf_op jit(solution)/shard_map/psum | solution.py:29
  103.3 97.2 %reduce-scatter.2.cloned.1.call-start = ((), (), s32[]{:S(2)}) async-start(), calls=%async_computation.4 | async-start | bytes 786432 | tf_op jit(solution)/shard_map/reduce_scatter | solution.py:38
  202.5 13.5 %all-to-all-start.1 = ((f32[32,1,2048]{2,1,0:T(1,128)}), f32[32,1,2048]{2,1,0:T(1,128)S(1)}, u32[]{:S(2)}, u32[]{:S(2)}) async-start(f32[32,1,2048]{2,1,0:T(1,128)} %copy.10), calls=%async_computation.2 | async-start | bytes 524288 | tf_op jit(solution)/shard_map/all_to_all | solution.py:39
Sparse Core Ops, SparseCore 0:
  103.5 37.3 all-reduce.1
  186.0 14.5 reduce-scatter.1
where the time goes:
time: 224 us
  matrix products  111 us (50%)
  waiting for transfers between devices  59.3 us (26%)
  blocking collectives  28.4 us (13%)
  between operations  14.1 us (6%)
  local copies, waits for them, and re-layouts  5.48 us (2%)
  starting transfers between devices  4.88 us (2%)
    dot_general x1, matrix products, contract_buses(): lax.dot_general(values, factors, (((1,), (1,)), ((), ())), precision=lax....  66.5 us
    dot_general x1, matrix products, on_device(): jnp.dot(group_slopes, shift_factors, precision=lax.Precision.HIGHEST, pre...  44.9 us
    psum x1, waiting for transfers between devices, on_device(): summed = lax.psum(partial_flows, 'bus')  37.3 us
    all_to_all x1, blocking collectives, on_device(): lax.all_to_all(widened, 'bus', split_axis=1, concat_axis=0, tiled=True)  18.5 us
    reduce_scatter x1, waiting for transfers between devices, on_device(): lax.psum_scatter(partial_grad, 'line', scatter_dimension=1, tiled=True)  14.7 us
    all_gather x1, blocking collectives, on_device(): widened = lax.all_gather(injections, 'line', axis=2, tiled=True)  9.91 us
    all_to_all x1, waiting for transfers between devices, on_device(): lax.all_to_all(reduced[:, None, :], 'bus', split_axis=0, concat_axis=1, t...  7.35 us
    all_to_all x1, starting transfers between devices, on_device(): lax.all_to_all(reduced[:, None, :], 'bus', split_axis=0, concat_axis=1, t...  4.62 us
  transfers between devices with their start and end apart: 3, of which 3 were waited for; matrix products, arithmetic and copies ran while one was open for 1% of the time, Pallas kernels for 0%

commit v1 on v0

v1 whole, which is shorter than its diff:
```python
import functools

import jax
import jax.numpy as jnp
from jax import lax
from jax.experimental import pallas as pl
from jax.experimental.pallas import tpu as pltpu
from jax.sharding import PartitionSpec as P

MESH = pl.DeviceIdType.MESH
F32 = jnp.float32
BF16 = jnp.bfloat16


def split(value):
    high = value.astype(BF16)
    return high, (value - high.astype(F32)).astype(BF16)


def dot_nt(a, b):
    return lax.dot_general(a, b, (((1,), (1,)), ((), ())), preferred_element_type=F32)


def dot_nn(a, b):
    return jnp.dot(a, b, preferred_element_type=F32)


def kernel(
    dims, inj, lim, cost, fac, flow_out, grad_out,
    snd, xbuf, xs, stage, fhi, flo, p, s_right, s_left, r_left, r_right,
    tot, ss, fsend, frecv, g, gc, hs, hx, own, gout,
    ld_sem, z_send, x_send, c_send, b_recv, right_send, left_send, left_recv, right_recv,
    f_send, f_recv, gc_send, gc_recv, hx_send, hx_recv, go_send, go_recv,
):
    nb, nl, ns, r, bx, lc, w, ch, nbuf, tw = dims
    z, x, c = lax.axis_index("bus"), lax.axis_index("line"), lax.axis_index("scen")
    kc, nch, nt = lc // w, lc // ch, bx // tw
    own_rows = nb * r
    rows = ns * own_rows

    def remote(src, dst, send, recv, where):
        return pltpu.make_async_remote_copy(
            src_ref=src, dst_ref=dst, send_sem=send, recv_sem=recv,
            device_id=where, device_id_type=MESH,
        )

    def load(i):
        start = pl.multiple_of(c * lc + i * ch, ch)
        slot = lax.rem(i, nbuf)
        return pltpu.make_async_copy(fac.at[pl.ds(start, ch), :], stage.at[slot], ld_sem.at[slot])

    for i in range(min(nbuf, nch)):
        load(jnp.int32(i)).start()

    barrier = pltpu.get_barrier_semaphore()
    for axis, here, count in (("bus", z, nb), ("line", x, nl), ("scen", c, ns)):
        for d in range(1, count):
            pl.semaphore_signal(
                barrier, inc=1, device_id={axis: lax.rem(here + d, count)}, device_id_type=MESH
            )

    for k in range(nb):
        snd[k] = inj[:, k, :]
    g[...] = jnp.zeros_like(g)
    pl.semaphore_wait(barrier, nb + nl + ns - 3)

    def block(xh, zz, cc):
        return xbuf.at[xh, pl.ds(pl.multiple_of((cc * nb + zz) * r, r), r), :]

    def over_bus(d):
        to = lax.rem(z + d, nb)
        return remote(snd.at[to], block(x, z, c), z_send.at[d], b_recv.at[x, z, c], {"bus": to})

    def over_line(dx, d):
        zz = lax.rem(z + nb - d, nb)
        return remote(
            block(x, zz, c), block(x, zz, c), x_send.at[dx, d], b_recv.at[x, zz, c],
            {"line": lax.rem(x + dx, nl)},
        )

    def over_core(dx, d, dc):
        zz, xh = lax.rem(z + nb - d, nb), lax.rem(x + nl - dx, nl)
        return remote(
            block(xh, zz, c), block(xh, zz, c), c_send.at[dx, d, dc], b_recv.at[xh, zz, c],
            {"scen": lax.rem(c + dc, ns)},
        )

    def arrived(xh, zz, cc):
        remote(
            block(xh, zz, cc), block(xh, zz, cc), z_send.at[0], b_recv.at[xh, zz, cc],
            {"bus": lax.rem(z + 1, nb)},
        ).wait_recv()

    for d in range(1, nb):
        over_bus(d).start()
    start_row = pl.multiple_of((c * nb + z) * r, r)
    xbuf[x, pl.ds(start_row, r), :] = snd[z]

    def forward(d):
        for dx in range(1, nl):
            over_line(dx, d).start()
        for dc in range(1, ns):
            over_core(0, d, dc).start()

    forward(0)

    def convert(i, carry):
        load(i).wait()
        slot = lax.rem(i, nbuf)
        high, low = split(stage[slot])
        at = pl.ds(pl.multiple_of(i * ch, ch), ch)
        fhi[at, :] = high
        flo[at, :] = low

        @pl.when(i + nbuf < nch)
        def _():
            load(i + nbuf).start()

        return carry

    for n in range(1, nb + 1):
        lax.fori_loop((n - 1) * nch // nb, n * nch // nb, convert, 0)
        if n < nb:
            arrived(x, lax.rem(z + nb - n, nb), c)
            forward(n)
        for dx in range(1, nl):
            xh, zz = lax.rem(x + nl - dx, nl), lax.rem(z + nb - n + 1, nb)
            arrived(xh, zz, c)
            for dc in range(1, ns):
                over_core(dx, n - 1, dc).start()

    for dc in range(1, ns):
        for dx in range(nl):
            for d in range(nb):
                arrived(lax.rem(x + nl - dx, nl), lax.rem(z + nb - d, nb), lax.rem(c + dc, ns))

    for xh in range(nl):
        high, low = split(xbuf[xh])
        xs[:rows, xh * bx:(xh + 1) * bx] = high
        xs[rows:, xh * bx:(xh + 1) * bx] = low

    def to_right(src, k):
        return remote(
            src.at[k], r_left.at[k], right_send.at[k], left_recv.at[k],
            {"bus": lax.rem(z + 1, nb)},
        )

    def to_left(src, k):
        return remote(
            src.at[k], r_right.at[k], left_send.at[k], right_recv.at[k],
            {"bus": lax.rem(z + nb - 1, nb)},
        )

    lag_left = jnp.minimum(2 * z, kc - 1)
    lag_right = jnp.minimum(2 * (nb - 1 - z), kc - 1)

    def relay(s):
        k = s - lag_left

        @pl.when((z > 0) & (k >= 0) & (k < kc))
        def _():
            to_right(s_right, k).wait_recv()

            @pl.when(z < nb - 1)
            def _():
                s_right[k] = r_left[k] + p[k]
                to_right(s_right, k).start()

        m = s - lag_right

        @pl.when((z < nb - 1) & (m >= 0) & (m < kc))
        def _():
            to_left(s_left, m).wait_recv()

            @pl.when(z > 0)
            def _():
                s_left[m] = r_right[m] + p[m]
                to_left(s_left, m).start()

    def lines_of(k):
        return pl.ds(pl.multiple_of(k * w, w), w)

    def forward_chunk(k, carry):
        both = dot_nt(xs[...], fhi[lines_of(k), :])
        p[k] = both[:rows] + both[rows:] + dot_nt(xs[:rows, :], flo[lines_of(k), :])

        @pl.when(z == 0)
        def _():
            to_right(p, k).start()

        @pl.when(z == nb - 1)
        def _():
            to_left(p, k).start()

        relay(k)
        return carry

    lax.fori_loop(0, kc, forward_chunk, 0)

    def slopes(k):
        tot[...] = p[k]

        @pl.when(z > 0)
        def _():
            tot[...] += r_left[k]

        @pl.when(z < nb - 1)
        def _():
            tot[...] += r_right[k]

        at = pl.ds(pl.multiple_of(c * lc + k * w, w), w)
        flow_out[:, at] = tot[pl.ds(pl.multiple_of((c * nb + z) * r, r), r), :]
        for dc in range(1, ns):
            other = lax.rem(c + dc, ns)
            fsend[dc - 1, :, lines_of(k)] = tot[pl.ds(pl.multiple_of((other * nb + z) * r, r), r), :]
        limits = lim[c * kc + k].astype(F32) / 100.0
        t = tot[...]
        slope = 2.0 * cost[c * kc + k] * (
            jnp.maximum(t - limits, 0.0) - jnp.maximum(-t - limits, 0.0)
        )
        high, low = split(slope)
        ss[:rows, :] = high
        ss[rows:, :] = low

    def backward_tile(k, col):
        cols = pl.ds(col, tw)
        both = dot_nn(ss[...], fhi[lines_of(k), cols])
        g[:, cols] += both[:rows] + both[rows:] + dot_nn(ss[:rows, :], flo[lines_of(k), cols])

    def backward_chunk(k, carry):
        relay(kc + k)
        slopes(k)

        def tile(t, carry2):
            backward_tile(k, pl.multiple_of(t * tw, tw))
            return carry2

        lax.fori_loop(0, nl * nt, tile, 0)
        return carry

    lax.fori_loop(0, kc - 1, backward_chunk, 0)
    last = kc - 1
    relay(jnp.int32(kc + last))
    slopes(last)

    def flows_over(dc):
        return remote(
            fsend.at[dc - 1], frecv.at[dc - 1], f_send.at[dc - 1], f_recv.at[dc - 1],
            {"scen": lax.rem(c + dc, ns)},
        )

    for dc in range(1, ns):
        flows_over(dc).start()

    order = [(dx, t) for dx in range(1, nl + 1) for t in range(nt)]

    def column(dx, t):
        return pl.multiple_of(lax.rem(x + dx, nl) * bx + t * tw, tw)

    def grad_core(i, dc):
        cols = pl.ds(column(*order[i]), tw)
        other = lax.rem(c + dc, ns)
        return remote(
            g.at[pl.ds(pl.multiple_of(other * own_rows, own_rows), own_rows), cols],
            gc.at[dc - 1, :, cols], gc_send.at[dc - 1, i], gc_recv.at[dc - 1, i], {"scen": other},
        )

    def grad_line(dx, t):
        cols = pl.ds(t * tw, tw)
        return remote(
            hs.at[dx - 1, :, cols], hx.at[dx - 1, :, cols],
            hx_send.at[dx - 1, t], hx_recv.at[dx - 1, t], {"line": lax.rem(x + dx, nl)},
        )

    def grad_bus(d, t):
        cols = pl.ds(t * tw, tw)
        to = lax.rem(z + d, nb)
        return remote(
            own.at[pl.ds(pl.multiple_of(to * r, r), r), cols],
            gout.at[pl.ds(pl.multiple_of(z * r, r), r), cols],
            go_send.at[d - 1, t], go_recv.at[d - 1, t], {"bus": to},
        )

    for i, (dx, t) in enumerate(order):
        backward_tile(last, column(dx, t))
        for dc in range(1, ns):
            grad_core(i, dc).start()

    mine = pl.ds(pl.multiple_of(c * own_rows, own_rows), own_rows)
    for i, (dx, t) in enumerate(order):
        cols = pl.ds(column(dx, t), tw)
        total = g[mine, cols]
        for dc in range(1, ns):
            grad_core(i, dc).wait_recv()
            total = total + gc[dc - 1, :, cols]
        if dx < nl:
            hs[dx - 1, :, t * tw:(t + 1) * tw] = total
            grad_line(dx, t).start()
        else:
            for e in range(1, nl):
                grad_line(e, t).wait_recv()
                total = total + hx[e - 1, :, t * tw:(t + 1) * tw]
            own[:, t * tw:(t + 1) * tw] = total
            for d in range(1, nb):
                grad_bus(d, t).start()

    for dc in range(1, ns):
        flows_over(dc).wait_recv()
        sender = lax.rem(c + ns - dc, ns)
        flow_out[:, pl.ds(pl.multiple_of(sender * lc, lc), lc)] = frecv[dc - 1]

    here = pl.ds(pl.multiple_of(z * r, r), r)
    gout[here, :] = own[here, :]

    for d in range(1, nb):
        over_bus(d).wait_send()
    for d in range(nb):
        for dx in range(1, nl):
            over_line(dx, d).wait_send()
        for dx in range(nl):
            for dc in range(1, ns):
                over_core(dx, d, dc).wait_send()

    def sent(k, carry):
        @pl.when(z < nb - 1)
        def _():
            to_right(p, k).wait_send()

        @pl.when(z > 0)
        def _():
            to_left(p, k).wait_send()

        return carry

    lax.fori_loop(0, kc, sent, 0)
    for dc in range(1, ns):
        flows_over(dc).wait_send()
        for i in range(len(order)):
            grad_core(i, dc).wait_send()
    for t in range(nt):
        for dx in range(1, nl):
            grad_line(dx, t).wait_send()
        for d in range(1, nb):
            grad_bus(d, t).wait_recv()
            grad_bus(d, t).wait_send()
    for k in range(nb):
        grad_out[:, k, :] = gout[k * r:(k + 1) * r, :]


def on_device(sizes, injections, shift_factors, line_limits, overload_cost):
    nb, nl, ns = sizes
    r, _, bx = injections.shape
    lines, buses = shift_factors.shape
    lc = lines // ns
    w = max(128, lc // 8)
    ch = w // 2
    nbuf = 4
    tw = max(128, bx // 2)
    kc, nt = lc // w, bx // tw
    own_rows = nb * r
    rows = ns * own_rows
    dims = (nb, nl, ns, r, bx, lc, w, ch, nbuf, tw)
    vmem, dma = pltpu.VMEM, pltpu.SemaphoreType.DMA
    whole = pl.BlockSpec(memory_space=pltpu.VMEM)
    return pl.pallas_call(
        functools.partial(kernel, dims),
        out_shape=(
            jax.ShapeDtypeStruct((r, lines), F32),
            jax.ShapeDtypeStruct((r, nb, bx), F32),
        ),
        in_specs=[whole, whole, whole, pl.BlockSpec(memory_space=pl.ANY)],
        out_specs=(whole, whole),
        scratch_shapes=[
            vmem((nb, r, bx), F32),
            vmem((nl, rows, bx), F32),
            vmem((2 * rows, buses), BF16),
            vmem((nbuf, ch, buses), F32),
            vmem((lc, buses), BF16),
            vmem((lc, buses), BF16),
            vmem((kc, rows, w), F32),
            vmem((kc, rows, w), F32),
            vmem((kc, rows, w), F32),
            vmem((kc, rows, w), F32),
            vmem((kc, rows, w), F32),
            vmem((rows, w), F32),
            vmem((2 * rows, w), BF16),
            vmem((ns - 1, r, lc), F32),
            vmem((ns - 1, r, lc), F32),
            vmem((rows, buses), F32),
            vmem((ns - 1, own_rows, buses), F32),
            vmem((nl - 1, own_rows, bx), F32),
            vmem((nl - 1, own_rows, bx), F32),
            vmem((own_rows, bx), F32),
            vmem((own_rows, bx), F32),
            dma((nbuf,)),
            dma((nb,)),
            dma((nl, nb)),
            dma((nl, nb, ns)),
            dma((nl, nb, ns)),
            dma((kc,)),
            dma((kc,)),
            dma((kc,)),
            dma((kc,)),
            dma((ns - 1,)),
            dma((ns - 1,)),
            dma((ns - 1, nl * nt)),
            dma((ns - 1, nl * nt)),
            dma((nl - 1, nt)),
            dma((nl - 1, nt)),
            dma((nb - 1, nt)),
            dma((nb - 1, nt)),
        ],
        compiler_params=pltpu.CompilerParams(
            collective_id=0, has_side_effects=True, vmem_limit_bytes=58 * 1024 * 1024
        ),
        cost_estimate=pl.CostEstimate(
            flops=12 * rows * lc * buses, bytes_accessed=4 * lc * buses, transcendentals=0
        ),
    )(
        injections,
        line_limits.reshape(ns * kc, 1, w),
        overload_cost.reshape(ns * kc, 1, w),
        shift_factors,
    )


def solution(mesh):
    sizes = tuple(mesh.shape[a] for a in ("bus", "line", "scen"))
    in_specs = (P(("grp", "bus", "scen"), None, "line"), P("line", "bus"), P("line"), P("line"))
    out_specs = (P(("grp", "bus", "scen"), "line"), P(("grp", "bus", "scen"), None, "line"))
    return jax.shard_map(
        functools.partial(on_device, sizes),
        mesh=mesh, in_specs=in_specs, out_specs=out_specs, check_vma=False,
    )
```

time: 224 us -> 62.9 us (0.28)
  matrix products: 111 us -> 0 us
  waiting for transfers between devices: 59.3 us -> 0 us
  Pallas kernels: 0 us -> 58.9 us
  blocking collectives: 28.4 us -> 0 us
  between operations: 14.1 us -> 0.64 us
  starting transfers between devices: 4.88 us -> 0 us
  local copies, waits for them, and re-layouts: 5.48 us -> 3.24 us
    dot_general x2 -> x0, matrix products: 111 us -> none  [the longest x1 66.5 us: contract_buses(): lax.dot_general(values, factors, (((1,), (1,)), ((), ())), precision=lax....]
    pallas_call x0 -> x1, Pallas kernels: none -> 58.9 us  [on_device(): pl.pallas_call(functools.partial(kernel, dims), out_shape=(jax.ShapeDtype...]
    psum x1 -> x0, waiting for transfers between devices: 37.3 us -> none  [on_device(): summed = lax.psum(partial_flows, 'bus')]
    all_to_all x1 -> x0, blocking collectives: 18.5 us -> none  [on_device(): lax.all_to_all(widened, 'bus', split_axis=1, concat_axis=0, tiled=True)]
    reduce_scatter x1 -> x0, waiting for transfers between devices: 14.7 us -> none  [on_device(): lax.psum_scatter(partial_grad, 'line', scatter_dimension=1, tiled=True)]
    all_gather x1 -> x0, blocking collectives: 9.91 us -> none  [on_device(): widened = lax.all_gather(injections, 'line', axis=2, tiled=True)]
    all_to_all x1 -> x0, waiting for transfers between devices: 7.35 us -> none  [on_device(): lax.all_to_all(reduced[:, None, :], 'bus', split_axis=0, concat_axis=1, t...]
    all_to_all x1 -> x0, starting transfers between devices: 4.62 us -> none  [on_device(): lax.all_to_all(reduced[:, None, :], 'bus', split_axis=0, concat_axis=1, t...]
  transfers between devices with their start and end apart: 3 -> 0, of which waited for: 3 -> 0; matrix products, arithmetic and copies ran while one was open for 1% -> 0% of each run, Pallas kernels for 0% -> 0%
where the time goes in v1:
time: 62.9 us; the launch traced here: 62.7 us
  Pallas kernels  58.9 us (94%)
  local copies, waits for them, and re-layouts  3.24 us (5%)
  between operations  0.64 us (1%)
    pallas_call x1, Pallas kernels, on_device(): pl.pallas_call(functools.partial(kernel, dims), out_shape=(jax.ShapeDtype...  58.9 us
    unnamed x2, local copies, waits for them, and re-layouts  3.24 us

profile of v1, /device:TPU:0, one launch (start us, length us, event | category | flops | bytes accessed | tf_op | source)
XLA Modules:
  0.0 62.7 jit_solution(10530673372042390756)
XLA Ops:
  0.6 58.9 %shard_map.59 = (f32[8,4096]{1,0:T(8,128)}, f32[8,4,2048]{2,1,0:T(4,128)}) custom-call(f32[8,4,2048]{2,1,0:T(4,128)} %inj.1, s32[16,1,256]{2,1,0:T(1,128)} %bitcast.2, f32[16,1,256]{2,1,0:T(1,128)} %bitcast.3, f32[4096,4096]{1,0:T(8,128)} %fac.1), custom_call_target="tpu_custom_call" | custom-call | flops 6442450944 | bytes 33554432 | tf_op jit(solution)/shard_map/pallas_call | solution.py:365
  59.5 1.6 %copy.8 = f32[8,4096]{1,0:T(8,128)} copy(f32[8,4096]{1,0:T(8,128)} %get-tuple-element.4) | data formatting | bytes 262144
  61.1 1.7 %copy.9 = f32[8,4,2048]{2,1,0:T(4,128)} copy(f32[8,4,2048]{2,1,0:T(4,128)} %get-tuple-element.5) | data formatting | bytes 524288

commit v2 on v1

--- a/solution.py
+++ b/solution.py
@@ -32,7 +32,7 @@
     ld_sem, z_send, x_send, c_send, b_recv, right_send, left_send, left_recv, right_recv,
     f_send, f_recv, gc_send, gc_recv, hx_send, hx_recv, go_send, go_recv,
 ):
-    nb, nl, ns, r, bx, lc, w, ch, nbuf, tw = dims
+    nb, nl, ns, r, bx, lc, w, ch, nbuf, tw, bt = dims
     z, x, c = lax.axis_index("bus"), lax.axis_index("line"), lax.axis_index("scen")
     kc, nch, nt = lc // w, lc // ch, bx // tw
     own_rows = nb * r
@@ -118,26 +118,48 @@
 
         return carry
 
+    def forward_line(d):
+        for dx in range(1, nl):
+            arrived(lax.rem(x + nl - dx, nl), lax.rem(z + nb - d, nb), c)
+            for dc in range(1, ns):
+                over_core(dx, d, dc).start()
+
+    def take(xh):
+        for dc in range(1, ns):
+            for d in range(nb):
+                arrived(xh, lax.rem(z + nb - d, nb), lax.rem(c + dc, ns))
+        cols = half(xh)
+        high, low = split(xbuf[xh])
+        xs[:rows, cols] = high
+        xs[rows:, cols] = low
+
+    def half(xh):
+        return pl.ds(pl.multiple_of(xh * bx, bx), bx)
+
+    def lines_of(k):
+        return pl.ds(pl.multiple_of(k * w, w), w)
+
+    def product(k, xh):
+        cols = half(xh)
+        both = dot_nt(xs[:, cols], fhi[lines_of(k), cols])
+        return both[:rows] + both[rows:] + dot_nt(xs[:rows, cols], flo[lines_of(k), cols])
+
+    def own_half(k, carry):
+        p[k] = product(k, x)
+        return carry
+
     for n in range(1, nb + 1):
         lax.fori_loop((n - 1) * nch // nb, n * nch // nb, convert, 0)
         if n < nb:
             arrived(x, lax.rem(z + nb - n, nb), c)
             forward(n)
-        for dx in range(1, nl):
-            xh, zz = lax.rem(x + nl - dx, nl), lax.rem(z + nb - n + 1, nb)
-            arrived(xh, zz, c)
-            for dc in range(1, ns):
-                over_core(dx, n - 1, dc).start()
-
-    for dc in range(1, ns):
-        for dx in range(nl):
-            for d in range(nb):
-                arrived(lax.rem(x + nl - dx, nl), lax.rem(z + nb - d, nb), lax.rem(c + dc, ns))
-
-    for xh in range(nl):
-        high, low = split(xbuf[xh])
-        xs[:rows, xh * bx:(xh + 1) * bx] = high
-        xs[rows:, xh * bx:(xh + 1) * bx] = low
+            forward_line(n - 1)
+    take(x)
+    lax.fori_loop(0, 1, own_half, 0)
+    forward_line(nb - 1)
+    lax.fori_loop(1, kc, own_half, 0)
+    for dx in range(1, nl):
+        take(lax.rem(x + dx, nl))
 
     def to_right(src, k):
         return remote(
@@ -151,8 +173,8 @@
             {"bus": lax.rem(z + nb - 1, nb)},
         )
 
-    lag_left = jnp.minimum(2 * z, kc - 1)
-    lag_right = jnp.minimum(2 * (nb - 1 - z), kc - 1)
+    lag_left, lag_right = 2 * z, 2 * (nb - 1 - z)
+    lag = jnp.maximum(lag_left, lag_right)
 
     def relay(s):
         k = s - lag_left
@@ -177,12 +199,9 @@
                 s_left[m] = r_right[m] + p[m]
                 to_left(s_left, m).start()
 
-    def lines_of(k):
-        return pl.ds(pl.multiple_of(k * w, w), w)
-
-    def forward_chunk(k, carry):
-        both = dot_nt(xs[...], fhi[lines_of(k), :])
-        p[k] = both[:rows] + both[rows:] + dot_nt(xs[:rows, :], flo[lines_of(k), :])
+    def forward_chunk(k):
+        for dx in range(1, nl):
+            p[k] += product(k, lax.rem(x + dx, nl))
 
         @pl.when(z == 0)
         def _():
@@ -191,11 +210,6 @@
         @pl.when(z == nb - 1)
         def _():
             to_left(p, k).start()
-
-        relay(k)
-        return carry
-
-    lax.fori_loop(0, kc, forward_chunk, 0)
 
     def slopes(k):
         tot[...] = p[k]
@@ -222,25 +236,35 @@
         ss[:rows, :] = high
         ss[rows:, :] = low
 
-    def backward_tile(k, col):
-        cols = pl.ds(col, tw)
+    def backward_tile(k, col, width):
+        cols = pl.ds(col, width)
         both = dot_nn(ss[...], fhi[lines_of(k), cols])
         g[:, cols] += both[:rows] + both[rows:] + dot_nn(ss[:rows, :], flo[lines_of(k), cols])
 
-    def backward_chunk(k, carry):
-        relay(kc + k)
-        slopes(k)
-
-        def tile(t, carry2):
-            backward_tile(k, pl.multiple_of(t * tw, tw))
-            return carry2
-
-        lax.fori_loop(0, nl * nt, tile, 0)
+    last = kc - 1
+
+    def step(s, carry):
+        @pl.when(2 * s < kc)
+        def _():
+            forward_chunk(2 * s)
+            forward_chunk(2 * s + 1)
+
+        relay(s)
+        k = s - lag
+
+        @pl.when((k >= 0) & (k < last))
+        def _():
+            slopes(k)
+
+            def tile(t, carry2):
+                backward_tile(k, pl.multiple_of(t * bt, bt), bt)
+                return carry2
+
+            lax.fori_loop(0, nl * bx // bt, tile, 0)
+
         return carry
 
-    lax.fori_loop(0, kc - 1, backward_chunk, 0)
-    last = kc - 1
-    relay(jnp.int32(kc + last))
+    lax.fori_loop(0, kc + 2 * (nb - 1), step, 0)
     slopes(last)
 
     def flows_over(dc):
@@ -282,7 +306,7 @@
         )
 
     for i, (dx, t) in enumerate(order):
-        backward_tile(last, column(dx, t))
+        backward_tile(last, column(dx, t), tw)
         for dc in range(1, ns):
             grad_core(i, dc).start()
 
@@ -354,12 +378,13 @@
     lc = lines // ns
     w = max(128, lc // 8)
     ch = w // 2
-    nbuf = 4
-    tw = max(128, bx // 2)
+    nbuf = 8
+    tw = max(128, bx // 4)
+    bt = max(128, bx // 2)
     kc, nt = lc // w, bx // tw
     own_rows = nb * r
     rows = ns * own_rows
-    dims = (nb, nl, ns, r, bx, lc, w, ch, nbuf, tw)
+    dims = (nb, nl, ns, r, bx, lc, w, ch, nbuf, tw, bt)
     vmem, dma = pltpu.VMEM, pltpu.SemaphoreType.DMA
     whole = pl.BlockSpec(memory_space=pltpu.VMEM)
     return pl.pallas_call(
@@ -411,7 +436,7 @@
             dma((nb - 1, nt)),
         ],
         compiler_params=pltpu.CompilerParams(
-            collective_id=0, has_side_effects=True, vmem_limit_bytes=58 * 1024 * 1024
+            collective_id=0, has_side_effects=True, vmem_limit_bytes=60 * 1024 * 1024
         ),
         cost_estimate=pl.CostEstimate(
             flops=12 * rows * lc * buses, bytes_accessed=4 * lc * buses, transcendentals=0

time: 62.9 us -> 68.9 us (1.095)
  Pallas kernels: 58.9 us -> 64.9 us
    pallas_call x1, Pallas kernels: 58.9 us -> 64.9 us  [on_device(): pl.pallas_call(functools.partial(kernel, dims), out_shape=(jax.ShapeDtype...]
where the time goes in v2:
time: 68.9 us; the launch traced here: 68.8 us
  Pallas kernels  64.9 us (94%)
  local copies, waits for them, and re-layouts  3.24 us (5%)
    pallas_call x1, Pallas kernels, on_device(): pl.pallas_call(functools.partial(kernel, dims), out_shape=(jax.ShapeDtype...  64.9 us
    unnamed x2, local copies, waits for them, and re-layouts  3.24 us

profile of v2, /device:TPU:0, one launch (start us, length us, event | category | flops | bytes accessed | tf_op | source)
XLA Modules:
  0.0 68.8 jit_solution(16145206340125379619)
XLA Ops:
  0.6 64.9 %shard_map.59 = (f32[8,4096]{1,0:T(8,128)}, f32[8,4,2048]{2,1,0:T(4,128)}) custom-call(f32[8,4,2048]{2,1,0:T(4,128)} %inj.1, s32[16,1,256]{2,1,0:T(1,128)} %bitcast.2, f32[16,1,256]{2,1,0:T(1,128)} %bitcast.3, f32[4096,4096]{1,0:T(8,128)} %fac.1), custom_call_target="tpu_custom_call" | custom-call | flops 6442450944 | bytes 33554432 | tf_op jit(solution)/shard_map/pallas_call | solution.py:390
  65.5 1.6 %copy.8 = f32[8,4096]{1,0:T(8,128)} copy(f32[8,4096]{1,0:T(8,128)} %get-tuple-element.4) | data formatting | bytes 262144
  67.1 1.7 %copy.9 = f32[8,4,2048]{2,1,0:T(4,128)} copy(f32[8,4,2048]{2,1,0:T(4,128)} %get-tuple-element.5) | data formatting | bytes 524288

commit v3 on v2

--- a/solution.py
+++ b/solution.py
@@ -144,8 +144,14 @@
         both = dot_nt(xs[:, cols], fhi[lines_of(k), cols])
         return both[:rows] + both[rows:] + dot_nt(xs[:rows, cols], flo[lines_of(k), cols])
 
+    hr = rows // 2
+
+    def put(k, value):
+        p[2 * k] = value[:hr]
+        p[2 * k + 1] = value[hr:]
+
     def own_half(k, carry):
-        p[k] = product(k, x)
+        put(k, product(k, x))
         return carry
 
     for n in range(1, nb + 1):
@@ -155,9 +161,10 @@
             forward(n)
             forward_line(n - 1)
     take(x)
-    lax.fori_loop(0, 1, own_half, 0)
+    first = kc // 2
+    lax.fori_loop(first, first + 1, own_half, 0)
     forward_line(nb - 1)
-    lax.fori_loop(1, kc, own_half, 0)
+    lax.fori_loop(first + 1, kc, own_half, 0)
     for dx in range(1, nl):
         take(lax.rem(x + dx, nl))
 
@@ -173,54 +180,78 @@
             {"bus": lax.rem(z + nb - 1, nb)},
         )
 
-    lag_left, lag_right = 2 * z, 2 * (nb - 1 - z)
-    lag = jnp.maximum(lag_left, lag_right)
+    lag_left = jnp.where(z == nb - 1, kc, jnp.minimum(2 * z, kc))
+    lag_right = jnp.where(z == 0, kc, jnp.minimum(2 * (nb - 1 - z), kc))
 
     def relay(s):
         k = s - lag_left
 
         @pl.when((z > 0) & (k >= 0) & (k < kc))
         def _():
-            to_right(s_right, k).wait_recv()
+            for h in range(2):
+                i = 2 * k + h
+                to_right(s_right, i).wait_recv()
+
+                @pl.when(z < nb - 1)
+                def _():
+                    s_right[i] = r_left[i] + p[i]
+                    to_right(s_right, i).start()
+
+        m = s - lag_right
+
+        @pl.when((z < nb - 1) & (m >= 0) & (m < kc))
+        def _():
+            for h in range(2):
+                i = 2 * m + h
+                to_left(s_left, i).wait_recv()
+
+                @pl.when(z > 0)
+                def _():
+                    s_left[i] = r_right[i] + p[i]
+                    to_left(s_left, i).start()
+
+    def send_ends(k):
+        for h in range(2):
+            @pl.when(z == 0)
+            def _():
+                to_right(p, 2 * k + h).start()
+
+            @pl.when(z == nb - 1)
+            def _():
+                to_left(p, 2 * k + h).start()
+
+    def whole_chunk(k, carry):
+        both = dot_nt(xs[...], fhi[lines_of(k), :])
+        put(k, both[:rows] + both[rows:] + dot_nt(xs[:rows, :], flo[lines_of(k), :]))
+        send_ends(k)
+        relay(k)
+        return carry
+
+    def rest_chunk(k, carry):
+        for dx in range(1, nl):
+            value = product(k, lax.rem(x + dx, nl))
+            p[2 * k] += value[:hr]
+            p[2 * k + 1] += value[hr:]
+        send_ends(k)
+        relay(k)
+        return carry
+
+    lax.fori_loop(0, first, whole_chunk, 0)
+    lax.fori_loop(first, kc, rest_chunk, 0)
+
+    def slopes(k):
+        for h in range(2):
+            i = 2 * k + h
+            part = pl.ds(h * hr, hr)
+            tot[part, :] = p[i]
+
+            @pl.when(z > 0)
+            def _():
+                tot[part, :] += r_left[i]
 
             @pl.when(z < nb - 1)
             def _():
-                s_right[k] = r_left[k] + p[k]
-                to_right(s_right, k).start()
-
-        m = s - lag_right
-
-        @pl.when((z < nb - 1) & (m >= 0) & (m < kc))
-        def _():
-            to_left(s_left, m).wait_recv()
-
-            @pl.when(z > 0)
-            def _():
-                s_left[m] = r_right[m] + p[m]
-                to_left(s_left, m).start()
-
-    def forward_chunk(k):
-        for dx in range(1, nl):
-            p[k] += product(k, lax.rem(x + dx, nl))
-
-        @pl.when(z == 0)
-        def _():
-            to_right(p, k).start()
-
-        @pl.when(z == nb - 1)
-        def _():
-            to_left(p, k).start()
-
-    def slopes(k):
-        tot[...] = p[k]
-
-        @pl.when(z > 0)
-        def _():
-            tot[...] += r_left[k]
-
-        @pl.when(z < nb - 1)
-        def _():
-            tot[...] += r_right[k]
+                tot[part, :] += r_right[i]
 
         at = pl.ds(pl.multiple_of(c * lc + k * w, w), w)
         flow_out[:, at] = tot[pl.ds(pl.multiple_of((c * nb + z) * r, r), r), :]
@@ -243,28 +274,19 @@
 
     last = kc - 1
 
-    def step(s, carry):
-        @pl.when(2 * s < kc)
-        def _():
-            forward_chunk(2 * s)
-            forward_chunk(2 * s + 1)
-
-        relay(s)
-        k = s - lag
-
-        @pl.when((k >= 0) & (k < last))
-        def _():
-            slopes(k)
-
-            def tile(t, carry2):
-                backward_tile(k, pl.multiple_of(t * bt, bt), bt)
-                return carry2
-
-            lax.fori_loop(0, nl * bx // bt, tile, 0)
-
-        return carry
-
-    lax.fori_loop(0, kc + 2 * (nb - 1), step, 0)
+    def backward_chunk(k, carry):
+        relay(kc + k)
+        slopes(k)
+
+        def tile(t, carry2):
+            backward_tile(k, pl.multiple_of(t * bt, bt), bt)
+            return carry2
+
+        lax.fori_loop(0, nl * bx // bt, tile, 0)
+        return carry
+
+    lax.fori_loop(0, last, backward_chunk, 0)
+    relay(jnp.int32(kc + last))
     slopes(last)
 
     def flows_over(dc):
@@ -356,7 +378,7 @@
 
         return carry
 
-    lax.fori_loop(0, kc, sent, 0)
+    lax.fori_loop(0, 2 * kc, sent, 0)
     for dc in range(1, ns):
         flows_over(dc).wait_send()
         for i in range(len(order)):
@@ -369,6 +391,15 @@
             grad_bus(d, t).wait_send()
     for k in range(nb):
         grad_out[:, k, :] = gout[k * r:(k + 1) * r, :]
+
+
+def hand_on(flows, grads, flows_out, grads_out, sem):
+    first = pltpu.make_async_copy(flows, flows_out, sem.at[0])
+    second = pltpu.make_async_copy(grads, grads_out, sem.at[1])
+    first.start()
+    second.start()
+    first.wait()
+    second.wait()
 
 
 def on_device(sizes, injections, shift_factors, line_limits, overload_cost):
@@ -387,7 +418,7 @@
     dims = (nb, nl, ns, r, bx, lc, w, ch, nbuf, tw, bt)
     vmem, dma = pltpu.VMEM, pltpu.SemaphoreType.DMA
     whole = pl.BlockSpec(memory_space=pltpu.VMEM)
-    return pl.pallas_call(
+    results = pl.pallas_call(
         functools.partial(kernel, dims),
         out_shape=(
             jax.ShapeDtypeStruct((r, lines), F32),
@@ -402,11 +433,11 @@
             vmem((nbuf, ch, buses), F32),
             vmem((lc, buses), BF16),
             vmem((lc, buses), BF16),
-            vmem((kc, rows, w), F32),
-            vmem((kc, rows, w), F32),
-            vmem((kc, rows, w), F32),
-            vmem((kc, rows, w), F32),
-            vmem((kc, rows, w), F32),
+            vmem((2 * kc, rows // 2, w), F32),
+            vmem((2 * kc, rows // 2, w), F32),
+            vmem((2 * kc, rows // 2, w), F32),
+            vmem((2 * kc, rows // 2, w), F32),
+            vmem((2 * kc, rows // 2, w), F32),
             vmem((rows, w), F32),
             vmem((2 * rows, w), BF16),
             vmem((ns - 1, r, lc), F32),
@@ -422,10 +453,10 @@
             dma((nl, nb)),
             dma((nl, nb, ns)),
             dma((nl, nb, ns)),
-            dma((kc,)),
-            dma((kc,)),
-            dma((kc,)),
-            dma((kc,)),
+            dma((2 * kc,)),
+            dma((2 * kc,)),
+            dma((2 * kc,)),
+            dma((2 * kc,)),
             dma((ns - 1,)),
             dma((ns - 1,)),
             dma((ns - 1, nl * nt)),
@@ -447,6 +478,14 @@
         overload_cost.reshape(ns * kc, 1, w),
         shift_factors,
     )
+    anywhere = pl.BlockSpec(memory_space=pl.ANY)
+    return pl.pallas_call(
+        hand_on,
+        out_shape=tuple(jax.ShapeDtypeStruct(a.shape, a.dtype) for a in results),
+        in_specs=[anywhere, anywhere],
+        out_specs=(anywhere, anywhere),
+        scratch_shapes=[dma((2,))],
+    )(*results)
 
 
 def solution(mesh):

time: 68.9 us -> 73.6 us (1.068)
  Pallas kernels: 64.9 us -> 72.8 us
  local copies, waits for them, and re-layouts: 3.24 us -> 0 us
    pallas_call x0 -> x1, Pallas kernels: none -> 13 us  [on_device(): pl.pallas_call(hand_on, out_shape=tuple((jax.ShapeDtypeStruct(a.shape, a....]
    pallas_call x1, Pallas kernels: 64.9 us -> 59.8 us  [on_device(): pl.pallas_call(functools.partial(kernel, dims), out_shape=(jax.ShapeDtype...]
    unnamed x2 -> x0, local copies, waits for them, and re-layouts: 3.24 us -> none
where the time goes in v3:
time: 73.6 us; the launch traced here: 73.4 us
  Pallas kernels  72.8 us (99%)
    pallas_call x1, Pallas kernels, on_device(): pl.pallas_call(functools.partial(kernel, dims), out_shape=(jax.ShapeDtype...  59.8 us
    pallas_call x1, Pallas kernels, on_device(): pl.pallas_call(hand_on, out_shape=tuple((jax.ShapeDtypeStruct(a.shape, a....  13 us

profile of v3, /device:TPU:0, one launch (start us, length us, event | category | flops | bytes accessed | tf_op | source)
XLA Modules:
  0.0 73.4 jit_solution(14136039695919134986)
XLA Ops:
  0.6 59.8 %shard_map.59 = (f32[8,4096]{1,0:T(8,128)}, f32[8,4,2048]{2,1,0:T(4,128)}) custom-call(f32[8,4,2048]{2,1,0:T(4,128)} %inj.1, s32[16,1,256]{2,1,0:T(1,128)} %bitcast.2, f32[16,1,256]{2,1,0:T(1,128)} %bitcast.3, f32[4096,4096]{1,0:T(8,128)} %fac.1), custom_call_target="tpu_custom_call" | custom-call | flops 6442450944 | bytes 33554432 | tf_op jit(solution)/shard_map/pallas_call | solution.py:421
  60.4 13.0 %shard_map.60 = (f32[8,4096]{1,0:T(8,128)}, f32[8,4,2048]{2,1,0:T(4,128)}) custom-call(f32[8,4096]{1,0:T(8,128)} %get-tuple-element.4.flows, f32[8,4,2048]{2,1,0:T(4,128)} %get-tuple-element.5.grads), custom_call_target="tpu_custom_call" | custom-call | tf_op jit(solution)/shard_map/pallas_call | solution.py:482

commit v4 on v1

--- a/solution.py
+++ b/solution.py
@@ -151,8 +151,8 @@
             {"bus": lax.rem(z + nb - 1, nb)},
         )
 
-    lag_left = jnp.minimum(2 * z, kc - 1)
-    lag_right = jnp.minimum(2 * (nb - 1 - z), kc - 1)
+    lag_left = jnp.where(z == nb - 1, kc, jnp.minimum(2 * z, kc - 1))
+    lag_right = jnp.where(z == 0, kc, jnp.minimum(2 * (nb - 1 - z), kc - 1))
 
     def relay(s):
         k = s - lag_left

time: 62.9 us -> 62 us (0.986)
  Pallas kernels: 58.9 us -> 57.9 us
    pallas_call x1, Pallas kernels: 58.9 us -> 57.9 us  [on_device(): pl.pallas_call(functools.partial(kernel, dims), out_shape=(jax.ShapeDtype...]
where the time goes in v4:
time: 62 us; the launch traced here: 61.8 us
  Pallas kernels  57.9 us (93%)
  local copies, waits for them, and re-layouts  3.24 us (5%)
  between operations  0.64 us (1%)
    pallas_call x1, Pallas kernels, on_device(): pl.pallas_call(functools.partial(kernel, dims), out_shape=(jax.ShapeDtype...  57.9 us
    unnamed x2, local copies, waits for them, and re-layouts  3.24 us

profile of v4, /device:TPU:0, one launch (start us, length us, event | category | flops | bytes accessed | tf_op | source)
XLA Modules:
  0.0 61.8 jit_solution(12058683912336371575)
XLA Ops:
  0.6 57.9 %shard_map.59 = (f32[8,4096]{1,0:T(8,128)}, f32[8,4,2048]{2,1,0:T(4,128)}) custom-call(f32[8,4,2048]{2,1,0:T(4,128)} %inj.1, s32[16,1,256]{2,1,0:T(1,128)} %bitcast.2, f32[16,1,256]{2,1,0:T(1,128)} %bitcast.3, f32[4096,4096]{1,0:T(8,128)} %fac.1), custom_call_target="tpu_custom_call" | custom-call | flops 6442450944 | bytes 33554432 | tf_op jit(solution)/shard_map/pallas_call | solution.py:365
  58.5 1.6 %copy.8 = f32[8,4096]{1,0:T(8,128)} copy(f32[8,4096]{1,0:T(8,128)} %get-tuple-element.4) | data formatting | bytes 262144
  60.1 1.7 %copy.9 = f32[8,4,2048]{2,1,0:T(4,128)} copy(f32[8,4,2048]{2,1,0:T(4,128)} %get-tuple-element.5) | data formatting | bytes 524288
